TPU v7x, 128 devices: a whole 4x4x4 slice. The times are simulated.
128 devices in a mesh: sp: 32 (over z, y, core), kv: 4 (over x).
Axes of the slice: x: 4, y: 4, z: 4, core: 2. Of those that a mesh axis runs over, the one named last changes fastest.
Arguments:
- query_states: bfloat16 [8192, 3584], P('sp', 'kv'), may hold values from -17 to 17
- key_states: bfloat16 [8192, 512], P('sp', 'kv'), may hold values from -17 to 17
- loader_value_rows: bfloat16 [8192, 512], P('sp', 'kv'), may hold values from -6 to 6
- group_sizes: int32 [16], replicated, may hold values from 1 to 8, 32 in all
- out_weight: bfloat16 [3584, 3584], P(None, 'kv'), may hold values from -0.09375 to 0.09375
Outputs:
- layer_output: bfloat16 [8192, 3584], P('sp', 'kv')
Inputs may be any that keep to these rules, and one draw needn't show every extreme that they name: `group_sizes`: the entries sum to 32, and the largest is exactly 8.
All inputs are finite; a program needn't handle non-finite values.
Results may differ from a plain program's by a relative error of at most 0.0055.
Values may be sent and summed in bfloat16 or wider, within the bound.
A program may use at most 192 MiB of HBM per device.

v0:
```python
import jax
import jax.numpy as jnp
from jax import lax
from jax.sharding import PartitionSpec as P


def passed_along(shard, axis, by):
    peers = lax.axis_size(axis)
    pairs = [(i, i + by) for i in range(peers) if 0 <= i + by < peers]
    return lax.ppermute(shard, axis, pairs)


def attend_tile(softmax_state, kv_piece, key_ids, query_heads, query_ids, seq_first):
    row_top, row_total, weighted = softmax_state
    head_width = query_heads.shape[2]
    scores = jnp.einsum(
        "qhd,kd->qhk", query_heads, kv_piece[0], preferred_element_type=jnp.float32
    ) * head_width ** (-0.5)
    visible = (key_ids[None, :] <= query_ids[:, None]) & (key_ids[None, :] >= seq_first)
    visible = visible[:, None, :]
    masked = jnp.where(visible, scores, -1e30)
    new_top = jnp.maximum(row_top, jnp.max(masked, axis=2))
    powers = jnp.where(visible, jnp.exp(masked - new_top[:, :, None]), 0.0)
    shrink = jnp.exp(row_top - new_top)
    row_total = row_total * shrink + jnp.sum(powers, axis=2)
    weighted = weighted * shrink[:, :, None] + jnp.einsum(
        "qhk,kd->qhd", powers.astype(jnp.bfloat16), kv_piece[1], preferred_element_type=jnp.float32
    )
    return (new_top, row_total, weighted)


def group_info(devices, group_sizes):
    group_ends = jnp.cumsum(group_sizes)
    group_begins = group_ends - group_sizes
    inside = (group_begins[None, :] <= devices[:, None]) & (devices[:, None] < group_ends[None, :])
    first_of = jnp.sum(jnp.where(inside, group_begins[None, :], 0), axis=1)
    size_of = jnp.sum(jnp.where(inside, group_sizes[None, :], 0), axis=1)
    return (first_of, size_of)


def on_device(query_states, key_states, loader_value_rows, group_sizes, out_weight):
    sp_count = lax.axis_size("sp")
    sp_index = lax.axis_index("sp")
    tok_count = query_states.shape[0]
    block_rows = tok_count // sp_count
    head_width = key_states.shape[1]
    query_cols = query_states.shape[1]
    query_split = query_states.reshape(sp_count, block_rows, query_cols)
    key_split = key_states.reshape(sp_count, block_rows, head_width)
    value_split = loader_value_rows.reshape(sp_count, block_rows, head_width)
    all_devices = lax.iota(jnp.int32, sp_count)
    dev_first, dev_size = group_info(all_devices, group_sizes)
    all_ids = lax.iota(jnp.int32, sp_count * tok_count)
    query_rows, key_rows, value_rows = (
        lax.all_to_all(query_split, "sp", split_axis=0, concat_axis=0, tiled=True),
        lax.all_to_all(key_split, "sp", split_axis=0, concat_axis=0, tiled=True),
        lax.all_to_all(value_split, "sp", split_axis=0, concat_axis=0, tiled=True),
    )
    query_heads = query_rows.reshape(tok_count, query_cols // head_width, head_width)
    kv_local = jnp.stack(
        [key_rows.reshape(tok_count, head_width), value_rows.reshape(tok_count, head_width)]
    )
    own_slot = jnp.clip(sp_index, 0, sp_count - 1).reshape(1)
    first_device = jnp.take(dev_first, own_slot)[0]
    group_offset = sp_index - first_device
    seq_first = first_device * tok_count
    query_ids = lax.dynamic_slice_in_dim(all_ids, sp_index * tok_count, tok_count)
    head_count = query_heads.shape[1]
    start_state = (
        jnp.full((tok_count, head_count), -1e30, jnp.float32),
        jnp.zeros((tok_count, head_count), jnp.float32),
        jnp.zeros((tok_count, head_count, head_width), jnp.float32),
    )

    def update(softmax_state, kv_piece, key_ids):
        return attend_tile(softmax_state, kv_piece, key_ids, query_heads, query_ids, seq_first)

    softmax_state = update(start_state, kv_local, query_ids)
    max_span = min(8, sp_count // 2)
    directions = (1,)
    sign = directions[0]
    travelling = kv_local
    for distance in range(1, max_span):
        travelling = passed_along(travelling, "sp", sign)
        source = jnp.clip(sp_index - sign * distance, 0, sp_count - 1)
        key_ids = lax.dynamic_slice_in_dim(all_ids, source * tok_count, tok_count)
        reach = distance <= group_offset
        softmax_state = lax.cond(
            reach,
            lambda current, piece=travelling, ids=key_ids: update(current, piece, ids),
            lambda current: current,
            softmax_state,
        )
    row_top, row_total, weighted = softmax_state
    attended = (
        (weighted / row_total[:, :, None]).astype(jnp.bfloat16).reshape(tok_count, query_cols)
    )
    returned = lax.all_to_all(
        attended.reshape(sp_count, block_rows, query_cols),
        "sp",
        split_axis=0,
        concat_axis=0,
        tiled=True,
    )
    returned = returned.reshape(tok_count, query_cols)
    projected = jnp.dot(
        lax.all_gather(returned, "kv", axis=1, tiled=True),
        out_weight,
        preferred_element_type=jnp.float32,
    )
    return projected.astype(jnp.bfloat16)


def solution(mesh):
    return jax.shard_map(
        on_device,
        mesh=mesh,
        in_specs=(P("sp", "kv"), P("sp", "kv"), P("sp", "kv"), P(), P(None, "kv")),
        out_specs=P("sp", "kv"),
        check_vma=False,
    )
```

profile of v0, /device:TPU:1, one launch (start us, length us, event | category | flops | bytes accessed | tf_op | source)
XLA Modules:
  0.0 158.9 jit_solution(5816176204264063267)
XLA Ops:
  6.5 9.6 %all-to-all-start.1 = ((bf16[32,8,128]{2,1,0:T(8,128)(2,1)}), bf16[32,8,128]{2,1,0:T(8,128)(2,1)S(1)}, u32[]{:S(2)}, u32[]{:S(2)}) async-start(bf16[32,8,128]{2,1,0:T(8,128)(2,1)} %bitcast.98), calls=%async_computation.1 | async-start | bytes 131072 | tf_op jit(solution)/shard_map/all_to_all | solution.py:56
  19.1 4.4 %all-to-all-done.1 = bf16[32,8,128]{2,1,0:T(8,128)(2,1)S(1)} async-done(((bf16[32,8,128]{2,1,0:T(8,128)(2,1)}), bf16[32,8,128]{2,1,0:T(8,128)(2,1)S(1)}, u32[]{:S(2)}, u32[]{:S(2)}) %all-to-all-start.1) | async-done | bytes 65568 | tf_op jit(solution)/shard_map/all_to_all | solution.py:56
  23.5 3.9 %all-to-all-start.2 = ((bf16[32,8,128]{2,1,0:T(8,128)(2,1)}), bf16[32,8,128]{2,1,0:T(8,128)(2,1)S(1)}, u32[]{:S(2)}, u32[]{:S(2)}) async-start(bf16[32,8,128]{2,1,0:T(8,128)(2,1)} %bitcast.99), calls=%async_computation.2 | async-start | bytes 131072 | tf_op jit(solution)/shard_map/all_to_all | solution.py:57
  27.4 7.4 %all-to-all-done.2 = bf16[32,8,128]{2,1,0:T(8,128)(2,1)S(1)} async-done(((bf16[32,8,128]{2,1,0:T(8,128)(2,1)}), bf16[32,8,128]{2,1,0:T(8,128)(2,1)S(1)}, u32[]{:S(2)}, u32[]{:S(2)}) %all-to-all-start.2) | async-done | bytes 65568 | tf_op jit(solution)/shard_map/all_to_all | solution.py:57
  34.8 3.9 %all-to-all-start = ((bf16[32,8,896]{2,1,0:T(8,128)(2,1)}), bf16[32,8,896]{2,1,0:T(8,128)(2,1)S(1)}, u32[]{:S(2)}, u32[]{:S(2)}) async-start(bf16[32,8,896]{2,1,0:T(8,128)(2,1)} %bitcast.95), calls=%async_computation | async-start | bytes 917504 | tf_op jit(solution)/shard_map/all_to_all | solution.py:55
  38.8 3.5 %collective-permute-start = (bf16[2,256,128]{2,1,0:T(8,128)(2,1)S(1)}, bf16[2,256,128]{2,1,0:T(8,128)(2,1)S(1)}, u32[]{:S(2)}, u32[]{:S(2)}) collective-permute-start(bf16[2,256,128]{2,1,0:T(8,128)(2,1)S(1)} %pad_maximum_fusion), channel_id=1, source_target_pairs={{0,4},{4,8},{8,12},{12,16},{16,20},{20,24},{24,28},{28,32},{32,36}... | collective-permute-start | bytes 393224 | tf_op jit(solution)/shard_map/ppermute | solution.py:10
  42.4 3.3 %collective-permute-done = bf16[2,256,128]{2,1,0:T(8,128)(2,1)S(1)} collective-permute-done((bf16[2,256,128]{2,1,0:T(8,128)(2,1)S(1)}, bf16[2,256,128]{2,1,0:T(8,128)(2,1)S(1)}, u32[]{:S(2)}, u32[]{:S(2)}) %collective-permute-start) | collective-permute-done | bytes 131104 | tf_op jit(solution)/shard_map/ppermute | solution.py:10
  45.7 4.4 %collective-permute-start.1 = (bf16[2,256,128]{2,1,0:T(8,128)(2,1)S(1)}, bf16[2,256,128]{2,1,0:T(8,128)(2,1)S(1)}, u32[]{:S(2)}, u32[]{:S(2)}) collective-permute-start(bf16[2,256,128]{2,1,0:T(8,128)(2,1)S(1)} %collective-permute-done), channel_id=1, source_target_pairs={{0,4},{4,8},{8,12},{12,16},{16,20},{20,24},{24,28},{28,32},{32,36}... | collective-permute-start | bytes 393224 | tf_op jit(solution)/shard_map/ppermute | solution.py:10
  50.1 1.9 %collective-permute-done.1 = bf16[2,256,128]{2,1,0:T(8,128)(2,1)S(1)} collective-permute-done((bf16[2,256,128]{2,1,0:T(8,128)(2,1)S(1)}, bf16[2,256,128]{2,1,0:T(8,128)(2,1)S(1)}, u32[]{:S(2)}, u32[]{:S(2)}) %collective-permute-start.1) | collective-permute-done | bytes 131104 | tf_op jit(solution)/shard_map/ppermute | solution.py:10
  52.0 4.3 %collective-permute-start.2 = (bf16[2,256,128]{2,1,0:T(8,128)(2,1)S(1)}, bf16[2,256,128]{2,1,0:T(8,128)(2,1)S(1)}, u32[]{:S(2)}, u32[]{:S(2)}) collective-permute-start(bf16[2,256,128]{2,1,0:T(8,128)(2,1)S(1)} %collective-permute-done.1), channel_id=1, source_target_pairs={{0,4},{4,8},{8,12},{12,16},{16,20},{20,24},{24,28},{28,32},{32,36}... | collective-permute-start | bytes 393224 | tf_op jit(solution)/shard_map/ppermute | solution.py:10
  57.3 0.9 collective-permute-done.2
  58.3 4.3 %collective-permute-start.3 = (bf16[2,256,128]{2,1,0:T(8,128)(2,1)S(1)}, bf16[2,256,128]{2,1,0:T(8,128)(2,1)S(1)}, u32[]{:S(2)}, u32[]{:S(2)}) collective-permute-start(bf16[2,256,128]{2,1,0:T(8,128)(2,1)S(1)} %collective-permute-done.2), channel_id=1, source_target_pairs={{0,4},{4,8},{8,12},{12,16},{16,20},{20,24},{24,28},{28,32},{32,36}... | collective-permute-start | bytes 393224 | tf_op jit(solution)/shard_map/ppermute | solution.py:10
  62.6 1.9 %collective-permute-done.3 = bf16[2,256,128]{2,1,0:T(8,128)(2,1)S(1)} collective-permute-done((bf16[2,256,128]{2,1,0:T(8,128)(2,1)S(1)}, bf16[2,256,128]{2,1,0:T(8,128)(2,1)S(1)}, u32[]{:S(2)}, u32[]{:S(2)}) %collective-permute-start.3) | collective-permute-done | bytes 131104 | tf_op jit(solution)/shard_map/ppermute | solution.py:10
  64.5 4.3 %collective-permute-start.4 = (bf16[2,256,128]{2,1,0:T(8,128)(2,1)S(1)}, bf16[2,256,128]{2,1,0:T(8,128)(2,1)S(1)}, u32[]{:S(2)}, u32[]{:S(2)}) collective-permute-start(bf16[2,256,128]{2,1,0:T(8,128)(2,1)S(1)} %collective-permute-done.3), channel_id=1, source_target_pairs={{0,4},{4,8},{8,12},{12,16},{16,20},{20,24},{24,28},{28,32},{32,36}... | collective-permute-start | bytes 393224 | tf_op jit(solution)/shard_map/ppermute | solution.py:10
  69.3 1.5 collective-permute-done.4
  70.8 4.3 %collective-permute-start.5 = (bf16[2,256,128]{2,1,0:T(8,128)(2,1)S(1)}, bf16[2,256,128]{2,1,0:T(8,128)(2,1)}, u32[]{:S(2)}, u32[]{:S(2)}) collective-permute-start(bf16[2,256,128]{2,1,0:T(8,128)(2,1)S(1)} %collective-permute-done.4), channel_id=1, source_target_pairs={{0,4},{4,8},{8,12},{12,16},{16,20},{20,24},{24,28},{28,32},{32,36}... | collective-permute-start | bytes 393224 | tf_op jit(solution)/shard_map/ppermute | solution.py:10
  75.2 1.9 %collective-permute-done.5 = bf16[2,256,128]{2,1,0:T(8,128)(2,1)} collective-permute-done((bf16[2,256,128]{2,1,0:T(8,128)(2,1)S(1)}, bf16[2,256,128]{2,1,0:T(8,128)(2,1)}, u32[]{:S(2)}, u32[]{:S(2)}) %collective-permute-start.5) | collective-permute-done | bytes 131104 | tf_op jit(solution)/shard_map/ppermute | solution.py:10
  77.1 4.4 %collective-permute-start.6 = (bf16[2,256,128]{2,1,0:T(8,128)(2,1)}, bf16[2,256,128]{2,1,0:T(8,128)(2,1)S(1)}, u32[]{:S(2)}, u32[]{:S(2)}) collective-permute-start(bf16[2,256,128]{2,1,0:T(8,128)(2,1)} %collective-permute-done.5), channel_id=1, source_target_pairs={{0,4},{4,8},{8,12},{12,16},{16,20},{20,24},{24,28},{28,32},{32,36}... | collective-permute-start | bytes 393224 | tf_op jit(solution)/shard_map/ppermute | solution.py:10
  81.5 0.9 convolution_add_fusion.7
  82.5 2.1 %conditional.7 = ((f32[256,7]{0,1:T(8,128)S(1)}, f32[256,7]{0,1:T(8,128)S(1)}, f32[256,7,128]{2,0,1:T(8,128)S(1)})) conditional(s32[]{:T(128)} %convert_element_type.59, (f32[256,7]{0,1:T(8,128)S(1)}, f32[256,7]{0,1:T(8,128)S(1)}, f32[256,7,128]{2,0,1:T(8,128)S(1)}) %tuple.57, (s32[256]{0:T(256)S(1)}, s32[256]{0:T(256)S(1)}, s32[]{:T(128)}, ...), branch_computations={%region_4.5_spmd, %region_5.8_spmd} | conditional | flops 241438464 | bytes 8377892 | solution.py:88
  83.6 1.0 convolution_add_fusion
  86.1 33.4 %all_to_all.20 = bf16[32,8,896]{2,1,0:T(8,128)(2,1)} all-to-all(bf16[32,8,896]{2,1,0:T(8,128)(2,1)S(1)} %reshape_reshape.3), channel_id=1, replica_groups=mesh['sp'=32,'kv'=4] {'sp'}, dimensions={0} | all-to-all | bytes 917504 | tf_op jit(solution)/shard_map/all_to_all | solution.py:98
  119.5 26.3 %all-gather.2.cloned.1.call-done = bf16[256,3584]{1,0:T(8,128)(2,1)} async-done(((bf16[256,896]{1,0:T(8,128)(2,1)}), bf16[256,3584]{1,0:T(8,128)(2,1)}) %all-gather.2.cloned.1.call-update) | async-done | bytes 1835024 | tf_op jit(solution)/shard_map/all_gather | solution.py:107
  145.8 6.2 %convolution_convert_fusion = bf16[256,896]{1,0:T(8,128)(2,1)} fusion(bf16[256,3584]{1,0:T(8,128)(2,1)} %all-gather.2.cloned.1.call-done, bf16[3584,896]{1,0:T(8,128)(2,1)} %param.23), kind=kOutput, calls=%fused_computation.174 | convolution fusion | flops 1644396544 | bytes 8716288 | tf_op jit(solution)/shard_map/dot_general | solution.py:106
  (42 shorter events, 6.4 us)
Async XLA Ops:
  6.5 16.9 %all-to-all-start.1 = ((bf16[32,8,128]{2,1,0:T(8,128)(2,1)}), bf16[32,8,128]{2,1,0:T(8,128)(2,1)S(1)}, u32[]{:S(2)}, u32[]{:S(2)}) async-start(bf16[32,8,128]{2,1,0:T(8,128)(2,1)} %bitcast.98), calls=%async_computation.1 | async-start | bytes 131072 | tf_op jit(solution)/shard_map/all_to_all | solution.py:56
  23.5 11.3 %all-to-all-start.2 = ((bf16[32,8,128]{2,1,0:T(8,128)(2,1)}), bf16[32,8,128]{2,1,0:T(8,128)(2,1)S(1)}, u32[]{:S(2)}, u32[]{:S(2)}) async-start(bf16[32,8,128]{2,1,0:T(8,128)(2,1)} %bitcast.99), calls=%async_computation.2 | async-start | bytes 131072 | tf_op jit(solution)/shard_map/all_to_all | solution.py:57
  34.8 21.5 %all-to-all-start = ((bf16[32,8,896]{2,1,0:T(8,128)(2,1)}), bf16[32,8,896]{2,1,0:T(8,128)(2,1)S(1)}, u32[]{:S(2)}, u32[]{:S(2)}) async-start(bf16[32,8,896]{2,1,0:T(8,128)(2,1)} %bitcast.95), calls=%async_computation | async-start | bytes 917504 | tf_op jit(solution)/shard_map/all_to_all | solution.py:55
  38.8 107.0 %all-gather.2.cloned.1.call-start = ((), (), s32[]{:S(2)}) async-start(), calls=%async_computation.4 | async-start | bytes 2293760 | tf_op jit(solution)/shard_map/all_gather | solution.py:107
  38.8 6.9 %collective-permute-start = (bf16[2,256,128]{2,1,0:T(8,128)(2,1)S(1)}, bf16[2,256,128]{2,1,0:T(8,128)(2,1)S(1)}, u32[]{:S(2)}, u32[]{:S(2)}) collective-permute-start(bf16[2,256,128]{2,1,0:T(8,128)(2,1)S(1)} %pad_maximum_fusion), channel_id=1, source_target_pairs={{0,4},{4,8},{8,12},{12,16},{16,20},{20,24},{24,28},{28,32},{32,36}... | collective-permute-start | bytes 393224 | tf_op jit(solution)/shard_map/ppermute | solution.py:10
  45.7 6.3 %collective-permute-start.1 = (bf16[2,256,128]{2,1,0:T(8,128)(2,1)S(1)}, bf16[2,256,128]{2,1,0:T(8,128)(2,1)S(1)}, u32[]{:S(2)}, u32[]{:S(2)}) collective-permute-start(bf16[2,256,128]{2,1,0:T(8,128)(2,1)S(1)} %collective-permute-done), channel_id=1, source_target_pairs={{0,4},{4,8},{8,12},{12,16},{16,20},{20,24},{24,28},{28,32},{32,36}... | collective-permute-start | bytes 393224 | tf_op jit(solution)/shard_map/ppermute | solution.py:10
  52.0 6.3 %collective-permute-start.2 = (bf16[2,256,128]{2,1,0:T(8,128)(2,1)S(1)}, bf16[2,256,128]{2,1,0:T(8,128)(2,1)S(1)}, u32[]{:S(2)}, u32[]{:S(2)}) collective-permute-start(bf16[2,256,128]{2,1,0:T(8,128)(2,1)S(1)} %collective-permute-done.1), channel_id=1, source_target_pairs={{0,4},{4,8},{8,12},{12,16},{16,20},{20,24},{24,28},{28,32},{32,36}... | collective-permute-start | bytes 393224 | tf_op jit(solution)/shard_map/ppermute | solution.py:10
  58.3 6.3 %collective-permute-start.3 = (bf16[2,256,128]{2,1,0:T(8,128)(2,1)S(1)}, bf16[2,256,128]{2,1,0:T(8,128)(2,1)S(1)}, u32[]{:S(2)}, u32[]{:S(2)}) collective-permute-start(bf16[2,256,128]{2,1,0:T(8,128)(2,1)S(1)} %collective-permute-done.2), channel_id=1, source_target_pairs={{0,4},{4,8},{8,12},{12,16},{16,20},{20,24},{24,28},{28,32},{32,36}... | collective-permute-start | bytes 393224 | tf_op jit(solution)/shard_map/ppermute | solution.py:10
  64.5 6.3 %collective-permute-start.4 = (bf16[2,256,128]{2,1,0:T(8,128)(2,1)S(1)}, bf16[2,256,128]{2,1,0:T(8,128)(2,1)S(1)}, u32[]{:S(2)}, u32[]{:S(2)}) collective-permute-start(bf16[2,256,128]{2,1,0:T(8,128)(2,1)S(1)} %collective-permute-done.3), channel_id=1, source_target_pairs={{0,4},{4,8},{8,12},{12,16},{16,20},{20,24},{24,28},{28,32},{32,36}... | collective-permute-start | bytes 393224 | tf_op jit(solution)/shard_map/ppermute | solution.py:10
  70.8 6.3 %collective-permute-start.5 = (bf16[2,256,128]{2,1,0:T(8,128)(2,1)S(1)}, bf16[2,256,128]{2,1,0:T(8,128)(2,1)}, u32[]{:S(2)}, u32[]{:S(2)}) collective-permute-start(bf16[2,256,128]{2,1,0:T(8,128)(2,1)S(1)} %collective-permute-done.4), channel_id=1, source_target_pairs={{0,4},{4,8},{8,12},{12,16},{16,20},{20,24},{24,28},{28,32},{32,36}... | collective-permute-start | bytes 393224 | tf_op jit(solution)/shard_map/ppermute | solution.py:10
  77.1 7.8 %collective-permute-start.6 = (bf16[2,256,128]{2,1,0:T(8,128)(2,1)}, bf16[2,256,128]{2,1,0:T(8,128)(2,1)S(1)}, u32[]{:S(2)}, u32[]{:S(2)}) collective-permute-start(bf16[2,256,128]{2,1,0:T(8,128)(2,1)} %collective-permute-done.5), channel_id=1, source_target_pairs={{0,4},{4,8},{8,12},{12,16},{16,20},{20,24},{24,28},{28,32},{32,36}... | collective-permute-start | bytes 393224 | tf_op jit(solution)/shard_map/ppermute | solution.py:10
Sparse Core Ops, SparseCore 0:
  119.6 26.1 all-gather.1
where the time goes:
time: 161 us; the launch traced here: 159 us
  waiting for transfers between devices  49.5 us (31%)
  starting transfers between devices  47.2 us (29%)
  blocking collectives  33.4 us (21%)
  between operations  14.3 us (9%)
  matrix products  9.02 us (6%)
  local copies, waits for them, and re-layouts  2.7 us (2%)
  other arithmetic  2.48 us (2%)
    all_to_all x1, blocking collectives, on_device(): lax.all_to_all(attended.reshape(sp_count, block_rows, query_cols), 'sp',...  33.4 us
    ppermute x7, starting transfers between devices, passed_along(): return lax.ppermute(shard, axis, pairs)  29.7 us
    all_gather x1, waiting for transfers between devices, on_device(): lax.all_gather(returned, 'kv', axis=1, tiled=True)  26.3 us
    ppermute x7, waiting for transfers between devices, passed_along(): return lax.ppermute(shard, axis, pairs)  11.4 us
    all_to_all x1, starting transfers between devices, on_device(): lax.all_to_all(key_split, 'sp', split_axis=0, concat_axis=0, tiled=True)  9.6 us
    all_to_all x1, waiting for transfers between devices, on_device(): lax.all_to_all(value_split, 'sp', split_axis=0, concat_axis=0, tiled=True)  7.42 us
    dot_general x1, matrix products, on_device(): jnp.dot(lax.all_gather(returned, 'kv', axis=1, tiled=True), out_weight, p...  6.22 us
    all_to_all x1, waiting for transfers between devices, on_device(): lax.all_to_all(key_split, 'sp', split_axis=0, concat_axis=0, tiled=True)  4.35 us
  transfers between devices with their start and end apart: 11, of which 9 were waited for; matrix products, arithmetic and copies ran while one was open for 4% of the time, Pallas kernels for 0%

commit v1 on v0

v1 whole, which is shorter than its diff:
```python
import functools

import jax
import jax.numpy as jnp
from jax import lax
from jax.experimental import pallas as pl
from jax.experimental.pallas import tpu as pltpu
from jax.sharding import PartitionSpec as P

MESH = pl.DeviceIdType.MESH
ROWS, FEAT, COLS, HEADS = 256, 128, 896, 7
PAIR = 16
KEYS = 512
LOG2E = 1.4426950408889634
CHUNKS = ((0, 64), (64, 64), (128, 64), (192, 64))
N_SEM = 128


def nxt(a, by):
    return lax.rem(a + by, 4)


def attention_kernel(
    q_ref, k_ref, v_ref, gs_ref, w_ref, o_ref,
    qv, kb, vb, xa, wv, acc, first, ssem, rsem, lsem,
):
    sp = lax.axis_index("sp")
    x = lax.axis_index("kv")
    c = lax.rem(sp, 2)
    y = lax.rem(sp // 2, 4)
    z = sp // 8

    def dev(z_, y_, c_, x_):
        return ((z_ * 4 + y_) * 2 + c_, x_)

    along_y = [dev(z, nxt(y, d), c, x) for d in (1, 3, 2)]
    along_z = [dev(nxt(z, d), y, c, x) for d in (1, 3, 2)]
    along_x = [dev(z, y, c, nxt(x, d)) for d in (1, 3, 2)]
    sibling = dev(z, y, 1 - c, x)

    peers = along_y + along_z + along_x + [sibling]
    barrier = pltpu.get_barrier_semaphore()
    for d in peers:
        pl.semaphore_signal(barrier, inc=1, device_id=d, device_id_type=MESH)
    pl.semaphore_wait(barrier, len(peers))

    ids = {}
    pending = []

    def remote(key, src, dst, d):
        i = ids.setdefault(key, len(ids))
        return pltpu.make_async_remote_copy(
            src_ref=src, dst_ref=dst, send_sem=ssem.at[i], recv_sem=rsem.at[i],
            device_id=d, device_id_type=MESH,
        )

    def send(key, src, dst, d):
        r = remote(key, src, dst, d)
        r.start()
        pending.append(r)

    def recv(key, dst):
        remote(key, dst, dst, sibling).wait_recv()

    src = {"k": k_ref, "v": v_ref}

    def shard(t, f, r0, n):
        if t == "k":
            return kb.at[z, f, c, pl.ds(r0, n)]
        return vb.at[f, y, c, pl.ds(r0, n)]

    def line(t, s, core, r0, n):
        if t == "k":
            return kb.at[s, :, core, pl.ds(r0, n)]
        return vb.at[:, s, core, pl.ds(r0, n)]

    def firsts(t):
        return (y, along_y) if t == "k" else (z, along_z)

    def seconds(t):
        return (z, along_z) if t == "k" else (y, along_y)

    def own_copy(t, ci):
        r0, n = CHUNKS[ci]
        f, _ = firsts(t)
        return pltpu.make_async_copy(
            src[t].at[pl.ds(r0, n)], shard(t, f, r0, n), lsem.at[2 * ci + (t == "v")]
        )

    def kv_first(ci):
        r0, n = CHUNKS[ci]
        for t in "kv":
            f, to = firsts(t)
            for i in range(3):
                send((t, ci, "f", i), src[t].at[pl.ds(r0, n)], shard(t, f, r0, n), to[i])
            own_copy(t, ci).start()

    def kv_second(ci):
        r0, n = CHUNKS[ci]
        for t in "kv":
            f, _ = firsts(t)
            s, to = seconds(t)
            for i, d in enumerate((3, 1, 2)):
                recv((t, ci, "f", i), shard(t, nxt(f, d), r0, n))
            own_copy(t, ci).wait()
            mine = line(t, s, c, r0, n)
            for i in range(3):
                send((t, ci, "s", i), mine, mine, to[i])
            send((t, ci, "c", 3), mine, mine, sibling)

    def kv_share(ci):
        r0, n = CHUNKS[ci]
        for i, d in enumerate((3, 1, 2)):
            for t in "kv":
                s, _ = seconds(t)
                got = line(t, nxt(s, d), c, r0, n)
                recv((t, ci, "s", i), got)
                send((t, ci, "c", i), got, got, sibling)

    def kv_ready(ci):
        r0, n = CHUNKS[ci]
        for i, d in enumerate((3, 1, 2, 0)):
            for t in "kv":
                s, _ = seconds(t)
                recv((t, ci, "c", i), line(t, nxt(s, d), 1 - c, r0, n))

    def halves(ci):
        r0, n = CHUNKS[ci]
        return pl.ds(r0, n // 2), pl.ds(r0 + n // 2, n // 2)

    def x_send(ci):
        a, b = halves(ci)
        right, left, _ = along_x
        send(("x", ci, "ra"), xa.at[0, a], xa.at[1, a], right)
        send(("x", ci, "lb"), xa.at[0, b], xa.at[2, b], left)
        send(("x", ci, "rb"), xa.at[0, b], xa.at[1, b], right)
        send(("x", ci, "la"), xa.at[0, a], xa.at[2, a], left)

    def x_forward(ci):
        a, b = halves(ci)
        right, left, _ = along_x
        recv(("x", ci, "ra"), xa.at[1, a])
        send(("x", ci, "fa"), xa.at[1, a], xa.at[3, a], right)
        recv(("x", ci, "lb"), xa.at[2, b])
        send(("x", ci, "fb"), xa.at[2, b], xa.at[3, b], left)

    def x_near(ci):
        a, b = halves(ci)
        recv(("x", ci, "rb"), xa.at[1, b])
        recv(("x", ci, "la"), xa.at[2, a])

    def x_far(ci):
        a, b = halves(ci)
        recv(("x", ci, "fa"), xa.at[3, a])
        recv(("x", ci, "fb"), xa.at[3, b])

    kv_first(0)
    q_copy = pltpu.make_async_copy(q_ref, qv, lsem.at[8])
    q_copy.start()
    for ci in range(1, len(CHUNKS)):
        kv_first(ci)
    w_copies = [
        pltpu.make_async_copy(
            w_ref.at[pl.ds(nxt(x, d) * COLS, COLS)], wv.at[i], lsem.at[9 + i]
        )
        for i, d in enumerate((0, 3, 1, 2))
    ]
    for w in w_copies:
        w.start()

    sizes = [gs_ref[i] for i in range(16)]

    @pl.loop(0, 32)
    def _(b):
        begin, total = 0, 0
        for size in sizes:
            begin = jnp.where(total <= b, total, begin)
            total = total + size
        first[b] = begin

    q_copy.wait()

    def attend(p, window):
        width = window * KEYS
        rows = pl.ds(pl.multiple_of(p * PAIR, PAIR), PAIR)
        q = jnp.concatenate([qv[rows, h * FEAT : (h + 1) * FEAT] for h in range(HEADS)], axis=0)
        lane = lax.broadcasted_iota(jnp.int32, (8, width), 1)
        sub = lax.broadcasted_iota(jnp.int32, (8, width), 0)
        key_id = (
            (lane // KEYS - (window - 1)) * KEYS
            + ((lane // 8) % 2) * 256 + ((lane % KEYS) // 16) * 8 + lane % 8
        )
        biases = []
        for half in range(2):
            low = first[2 * p + half] * 256 - p * KEYS
            high = half * 256 + sp * 8 + sub
            biases.append(jnp.where((key_id >= low) & (key_id <= high), 0.0, -1e30))
        bias = jnp.stack(biases)
        parts = []
        for j in range(window):
            at = pl.ds(pl.multiple_of((p - (window - 1) + j) * PAIR, PAIR), PAIR)
            keys = kb[:, :, :, at, :].reshape(KEYS, FEAT)
            parts.append(
                lax.dot_general(q, keys, (((1,), (1,)), ((), ())), preferred_element_type=jnp.float32)
            )
        scores = jnp.concatenate(parts, axis=1) if window > 1 else parts[0]
        scores = scores * (LOG2E * FEAT**-0.5)
        scores = (scores.reshape(HEADS, 2, 8, width) + bias[None]).reshape(HEADS * PAIR, width)
        top = jnp.max(scores, axis=1, keepdims=True)
        powers = jnp.exp2(scores - top)
        total = jnp.sum(powers, axis=1, keepdims=True)
        powers = powers.astype(jnp.bfloat16)
        out = jnp.zeros((HEADS * PAIR, FEAT), jnp.float32)
        for j in range(window):
            at = pl.ds(pl.multiple_of((p - (window - 1) + j) * PAIR, PAIR), PAIR)
            values = vb[:, :, :, at, :].reshape(KEYS, FEAT)
            out = out + jnp.dot(
                powers[:, j * KEYS : (j + 1) * KEYS], values, preferred_element_type=jnp.float32
            )
        out = (out / total).astype(jnp.bfloat16)
        for h in range(HEADS):
            xa[0, rows, h * FEAT : (h + 1) * FEAT] = out[h * PAIR : (h + 1) * PAIR]

    def attend_chunk(ci):
        r0, n = CHUNKS[ci]
        if ci == 0:
            for p in range(n // PAIR):
                attend(p, p + 1)
        else:
            @pl.loop(r0 // PAIR, (r0 + n) // PAIR)
            def _(p):
                attend(p, 5)

    def project(slot, r0, n, start=False):
        part = jnp.dot(xa[slot, r0 : r0 + n], wv[slot], preferred_element_type=jnp.float32)
        if start:
            acc[r0 : r0 + n] = part
        else:
            acc[r0 : r0 + n] += part

    kv_second(0)
    kv_second(1)
    kv_share(0)
    kv_second(2)
    kv_ready(0)
    attend_chunk(0)
    x_send(0)
    kv_second(3)
    kv_share(1)
    kv_ready(1)
    attend_chunk(1)
    x_send(1)
    kv_share(2)
    x_forward(0)
    kv_ready(2)
    attend_chunk(2)
    x_send(2)
    kv_share(3)
    x_forward(1)
    kv_ready(3)
    attend_chunk(3)
    x_send(3)
    for w in w_copies:
        w.wait()
    project(0, 0, 128, start=True)
    x_forward(2)
    project(0, 128, 128, start=True)
    x_near(0)
    x_near(1)
    project(1, 0, 128)
    x_forward(3)
    project(2, 0, 128)
    x_far(0)
    x_far(1)
    project(3, 0, 128)
    x_near(2)
    x_near(3)
    project(1, 128, 128)
    project(2, 128, 128)
    x_far(2)
    x_far(3)
    project(3, 128, 128)
    o_ref[...] = acc[...].astype(jnp.bfloat16)
    for r in pending:
        r.wait_send()


def on_device(query_states, key_states, loader_value_rows, group_sizes, out_weight):
    anywhere = pl.BlockSpec(memory_space=pl.ANY)
    gathered = pltpu.VMEM((4, 4, 2, ROWS, FEAT), jnp.bfloat16)
    return pl.pallas_call(
        attention_kernel,
        out_shape=jax.ShapeDtypeStruct((ROWS, COLS), jnp.bfloat16),
        in_specs=[anywhere, anywhere, anywhere, pl.BlockSpec(memory_space=pltpu.SMEM), anywhere],
        out_specs=pl.BlockSpec(memory_space=pltpu.VMEM),
        scratch_shapes=[
            pltpu.VMEM((ROWS, COLS), jnp.bfloat16),
            gathered,
            gathered,
            pltpu.VMEM((4, ROWS, COLS), jnp.bfloat16),
            pltpu.VMEM((4, COLS, COLS), jnp.bfloat16),
            pltpu.VMEM((ROWS, COLS), jnp.float32),
            pltpu.SMEM((32,), jnp.int32),
            pltpu.SemaphoreType.DMA((N_SEM,)),
            pltpu.SemaphoreType.DMA((N_SEM,)),
            pltpu.SemaphoreType.DMA((16,)),
        ],
        compiler_params=pltpu.CompilerParams(
            collective_id=0, has_side_effects=True, vmem_limit_bytes=56 << 20
        ),
    )(query_states, key_states, loader_value_rows, group_sizes, out_weight)


def solution(mesh):
    return jax.shard_map(
        on_device,
        mesh=mesh,
        in_specs=(P("sp", "kv"), P("sp", "kv"), P("sp", "kv"), P(), P(None, "kv")),
        out_specs=P("sp", "kv"),
        check_vma=False,
    )
```

time: 161 us -> 47.6 us (0.30)
  waiting for transfers between devices: 49.5 us -> 0 us
  starting transfers between devices: 47.2 us -> 0 us
  Pallas kernels: 0 us -> 45 us
  blocking collectives: 33.4 us -> 0 us
  between operations: 14.3 us -> 0.01 us
  matrix products: 9.02 us -> 0 us
  other arithmetic: 2.48 us -> 0 us
    pallas_call x0 -> x1, Pallas kernels: none -> 45 us  [on_device(): pl.pallas_call(attention_kernel, out_shape=jax.ShapeDtypeStruct((ROWS, CO...]
    all_to_all x1 -> x0, blocking collectives: 33.4 us -> none  [on_device(): lax.all_to_all(attended.reshape(sp_count, block_rows, query_cols), 'sp',...]
    ppermute x7 -> x0, starting transfers between devices: 29.7 us -> none  [passed_along(): return lax.ppermute(shard, axis, pairs)]
    all_gather x1 -> x0, waiting for transfers between devices: 26.3 us -> none  [on_device(): lax.all_gather(returned, 'kv', axis=1, tiled=True)]
    all_to_all x3 -> x0, starting transfers between devices: 17.4 us -> none  [the longest x1 9.6 us: on_device(): lax.all_to_all(key_split, 'sp', split_axis=0, concat_axis=0, tiled=True)]
    all_to_all x3 -> x0, waiting for transfers between devices: 11.8 us -> none  [the longest x1 7.42 us: on_device(): lax.all_to_all(value_split, 'sp', split_axis=0, concat_axis=0, tiled=True)]
    ppermute x7 -> x0, waiting for transfers between devices: 11.4 us -> none  [passed_along(): return lax.ppermute(shard, axis, pairs)]
    dot_general x5 -> x0, matrix products: 9.02 us -> none  [the longest x1 6.22 us: on_device(): jnp.dot(lax.all_gather(returned, 'kv', axis=1, tiled=True), out_weight, p...]
  transfers between devices with their start and end apart: 11 -> 0, of which waited for: 9 -> 0; matrix products, arithmetic and copies ran while one was open for 4% -> 0% of each run, Pallas kernels for 0% -> 0%
where the time goes in v1:
time: 47.6 us; the launch traced here: 46.8 us
  Pallas kernels  45 us (95%)
  local copies, waits for them, and re-layouts  1.82 us (4%)
    pallas_call x1, Pallas kernels, on_device(): pl.pallas_call(attention_kernel, out_shape=jax.ShapeDtypeStruct((ROWS, CO...  45 us
    unnamed x1, local copies, waits for them, and re-layouts  1.82 us

profile of v1, /device:TPU:1, one launch (start us, length us, event | category | flops | bytes accessed | tf_op | source)
XLA Modules:
  0.0 46.8 jit_solution(12956764299820730188)
XLA Ops:
  0.0 45.0 %shard_map.55 = bf16[256,896]{1,0:T(8,128)(2,1)} custom-call(bf16[256,896]{1,0:T(8,128)(2,1)} %q_ref.1, bf16[256,128]{1,0:T(8,128)(2,1)} %k_ref.1, bf16[256,128]{1,0:T(8,128)(2,1)} %v_ref.1, s32[16]{0:T(128)} %gs_ref.1, bf16[3584,896]{1,0:T(8,128)(2,1)} %w_ref.1), custom_call_target="tpu_custom_call" | custom-call | tf_op jit(solution)/shard_map/pallas_call | solution.py:291
  45.0 1.8 %copy.7 = bf16[256,896]{1,0:T(8,128)(2,1)} copy(bf16[256,896]{1,0:T(8,128)(2,1)} %shard_map.55) | data formatting | bytes 917504

commit v2 on v1

--- a/solution.py
+++ b/solution.py
@@ -12,17 +12,24 @@
 PAIR = 16
 KEYS = 512
 LOG2E = 1.4426950408889634
+QUAD = 32
 CHUNKS = ((0, 64), (64, 64), (128, 64), (192, 64))
-N_SEM = 128
+N_SEM = 26 * len(CHUNKS)
+SCALE = LOG2E * FEAT**-0.5
+NT = (((1,), (1,)), ((), ()))
 
 
 def nxt(a, by):
     return lax.rem(a + by, 4)
 
 
+def by_lanes(op, a):
+    return op(op(a[:, :128], a[:, 128:256]), op(a[:, 256:384], a[:, 384:]))
+
+
 def attention_kernel(
     q_ref, k_ref, v_ref, gs_ref, w_ref, o_ref,
-    qv, kb, vb, xa, wv, acc, first, ssem, rsem, lsem,
+    qv, kb, vb, xa, wv, acc, ov, sizes, first, ssem, rsem, lsem,
 ):
     sp = lax.axis_index("sp")
     x = lax.axis_index("kv")
@@ -42,6 +49,18 @@
     barrier = pltpu.get_barrier_semaphore()
     for d in peers:
         pl.semaphore_signal(barrier, inc=1, device_id=d, device_id_type=MESH)
+    size_copy = pltpu.make_async_copy(gs_ref, sizes, lsem.at[0])
+    size_copy.start()
+    q_copy = pltpu.make_async_copy(q_ref, qv, lsem.at[1])
+    q_copy.start()
+    w_copies = [
+        pltpu.make_async_copy(
+            w_ref.at[pl.ds(nxt(x, d) * COLS, COLS)], wv.at[i], lsem.at[2 + i]
+        )
+        for i, d in enumerate((0, 3, 1, 2))
+    ]
+    for w in w_copies:
+        w.start()
     pl.semaphore_wait(barrier, len(peers))
 
     ids = {}
@@ -84,7 +103,7 @@
         r0, n = CHUNKS[ci]
         f, _ = firsts(t)
         return pltpu.make_async_copy(
-            src[t].at[pl.ds(r0, n)], shard(t, f, r0, n), lsem.at[2 * ci + (t == "v")]
+            src[t].at[pl.ds(r0, n)], shard(t, f, r0, n), lsem.at[8 + 2 * ci + (t == "v")]
         )
 
     def kv_first(ci):
@@ -154,82 +173,90 @@
         recv(("x", ci, "fa"), xa.at[3, a])
         recv(("x", ci, "fb"), xa.at[3, b])
 
-    kv_first(0)
-    q_copy = pltpu.make_async_copy(q_ref, qv, lsem.at[8])
-    q_copy.start()
-    for ci in range(1, len(CHUNKS)):
-        kv_first(ci)
-    w_copies = [
-        pltpu.make_async_copy(
-            w_ref.at[pl.ds(nxt(x, d) * COLS, COLS)], wv.at[i], lsem.at[9 + i]
-        )
-        for i, d in enumerate((0, 3, 1, 2))
-    ]
-    for w in w_copies:
-        w.start()
-
-    sizes = [gs_ref[i] for i in range(16)]
-
-    @pl.loop(0, 32)
-    def _(b):
-        begin, total = 0, 0
-        for size in sizes:
-            begin = jnp.where(total <= b, total, begin)
-            total = total + size
-        first[b] = begin
-
-    q_copy.wait()
-
-    def attend(p, window):
-        width = window * KEYS
-        rows = pl.ds(pl.multiple_of(p * PAIR, PAIR), PAIR)
-        q = jnp.concatenate([qv[rows, h * FEAT : (h + 1) * FEAT] for h in range(HEADS)], axis=0)
-        lane = lax.broadcasted_iota(jnp.int32, (8, width), 1)
-        sub = lax.broadcasted_iota(jnp.int32, (8, width), 0)
-        key_id = (
-            (lane // KEYS - (window - 1)) * KEYS
-            + ((lane // 8) % 2) * 256 + ((lane % KEYS) // 16) * 8 + lane % 8
-        )
+    def make_table():
+        size_copy.wait()
+        listed = [sizes[i] for i in range(16)]
+
+        @pl.loop(0, 32)
+        def _(b):
+            begin, total = 0, 0
+            for size in listed:
+                begin = jnp.where(total <= b, total, begin)
+                total = total + size
+            first[b] = begin
+
+    def pair_rows(p):
+        return pl.ds(p * PAIR, PAIR)
+
+    def gathered(ref, p):
+        return ref[:, :, :, pair_rows(p), :].reshape(KEYS, FEAT)
+
+    def pair_bias(p, kp):
+        lane = lax.broadcasted_iota(jnp.int32, (8, KEYS), 1)
+        sub = lax.broadcasted_iota(jnp.int32, (8, KEYS), 0)
+        key_id = kp * KEYS + ((lane // 8) % 2) * 256 + (lane // 16) * 8 + lane % 8
         biases = []
         for half in range(2):
-            low = first[2 * p + half] * 256 - p * KEYS
-            high = half * 256 + sp * 8 + sub
-            biases.append(jnp.where((key_id >= low) & (key_id <= high), 0.0, -1e30))
-        bias = jnp.stack(biases)
-        parts = []
-        for j in range(window):
-            at = pl.ds(pl.multiple_of((p - (window - 1) + j) * PAIR, PAIR), PAIR)
-            keys = kb[:, :, :, at, :].reshape(KEYS, FEAT)
-            parts.append(
-                lax.dot_general(q, keys, (((1,), (1,)), ((), ())), preferred_element_type=jnp.float32)
+            seen = key_id >= first[2 * p + half] * 256
+            if kp == p:
+                seen = seen & (key_id <= p * KEYS + half * 256 + sp * 8 + sub)
+            biases.append(jnp.where(seen, 0.0, -1e30))
+        return jnp.stack(biases)
+
+    def scored(q, p_list, kp):
+        s = lax.dot_general(q, gathered(kb, kp), NT, preferred_element_type=jnp.float32)
+        bias = jnp.stack([pair_bias(p, kp)[None] for p in p_list])
+        return (s.reshape(len(p_list), HEADS, 2, 8, KEYS) + bias).reshape(s.shape)
+
+    def attend(t):
+        m = HEADS * PAIR
+        p0, p1 = 2 * t, 2 * t + 1
+        q = jnp.concatenate(
+            [qv[pair_rows(p), h * FEAT : (h + 1) * FEAT] for p in (p0, p1) for h in range(HEADS)], axis=0
+        )
+        middle = range(max(0, p0 - 3), p0 + 1)
+        both = [scored(q, (p0, p1), kp) for kp in middle]
+        edge1 = scored(q[m:], (p1,), p1)
+        top1 = by_lanes(jnp.maximum, edge1)
+        edge0 = None
+        if p0 >= 4:
+            edge0 = scored(q[:m], (p0,), p0 - 4)
+            tops = jnp.concatenate([by_lanes(jnp.maximum, edge0), top1], axis=0)
+        else:
+            tops = jnp.concatenate([jnp.full((m, 128), -1e30, jnp.float32), top1], axis=0)
+        for s in both:
+            tops = jnp.maximum(tops, by_lanes(jnp.maximum, s))
+        top = jnp.max(tops, axis=1, keepdims=True) * SCALE
+        powers = jnp.exp2(edge1 * SCALE - top[m:])
+        total1 = by_lanes(jnp.add, powers)
+        out1 = jnp.dot(powers.astype(jnp.bfloat16), gathered(vb, p1), preferred_element_type=jnp.float32)
+        if edge0 is not None:
+            powers = jnp.exp2(edge0 * SCALE - top[:m])
+            total0 = by_lanes(jnp.add, powers)
+            out0 = jnp.dot(
+                powers.astype(jnp.bfloat16), gathered(vb, p0 - 4), preferred_element_type=jnp.float32
             )
-        scores = jnp.concatenate(parts, axis=1) if window > 1 else parts[0]
-        scores = scores * (LOG2E * FEAT**-0.5)
-        scores = (scores.reshape(HEADS, 2, 8, width) + bias[None]).reshape(HEADS * PAIR, width)
-        top = jnp.max(scores, axis=1, keepdims=True)
-        powers = jnp.exp2(scores - top)
-        total = jnp.sum(powers, axis=1, keepdims=True)
-        powers = powers.astype(jnp.bfloat16)
-        out = jnp.zeros((HEADS * PAIR, FEAT), jnp.float32)
-        for j in range(window):
-            at = pl.ds(pl.multiple_of((p - (window - 1) + j) * PAIR, PAIR), PAIR)
-            values = vb[:, :, :, at, :].reshape(KEYS, FEAT)
+        else:
+            total0 = jnp.zeros((m, 128), jnp.float32)
+            out0 = jnp.zeros((m, FEAT), jnp.float32)
+        total = jnp.concatenate([total0, total1], axis=0)
+        out = jnp.concatenate([out0, out1], axis=0)
+        for s, kp in zip(both, middle):
+            powers = jnp.exp2(s * SCALE - top)
+            total = total + by_lanes(jnp.add, powers)
             out = out + jnp.dot(
-                powers[:, j * KEYS : (j + 1) * KEYS], values, preferred_element_type=jnp.float32
+                powers.astype(jnp.bfloat16), gathered(vb, kp), preferred_element_type=jnp.float32
             )
-        out = (out / total).astype(jnp.bfloat16)
-        for h in range(HEADS):
-            xa[0, rows, h * FEAT : (h + 1) * FEAT] = out[h * PAIR : (h + 1) * PAIR]
+        out = (out / jnp.sum(total, axis=1, keepdims=True)).astype(jnp.bfloat16)
+        for i, p in enumerate((p0, p1)):
+            for h in range(HEADS):
+                at = i * m + h * PAIR
+                xa[0, pair_rows(p), h * FEAT : (h + 1) * FEAT] = out[at : at + PAIR]
 
     def attend_chunk(ci):
         r0, n = CHUNKS[ci]
-        if ci == 0:
-            for p in range(n // PAIR):
-                attend(p, p + 1)
-        else:
-            @pl.loop(r0 // PAIR, (r0 + n) // PAIR)
-            def _(p):
-                attend(p, 5)
+        for t in range(r0 // QUAD, (r0 + n) // QUAD):
+            attend(t)
 
     def project(slot, r0, n, start=False):
         part = jnp.dot(xa[slot, r0 : r0 + n], wv[slot], preferred_element_type=jnp.float32)
@@ -238,49 +265,58 @@
         else:
             acc[r0 : r0 + n] += part
 
-    kv_second(0)
-    kv_second(1)
-    kv_share(0)
-    kv_second(2)
-    kv_ready(0)
-    attend_chunk(0)
-    x_send(0)
-    kv_second(3)
-    kv_share(1)
-    kv_ready(1)
-    attend_chunk(1)
-    x_send(1)
-    kv_share(2)
-    x_forward(0)
-    kv_ready(2)
-    attend_chunk(2)
-    x_send(2)
-    kv_share(3)
-    x_forward(1)
-    kv_ready(3)
-    attend_chunk(3)
-    x_send(3)
+    out_copies = []
+
+    def put_out(r0, n):
+        ov[r0 : r0 + n] = acc[r0 : r0 + n].astype(jnp.bfloat16)
+        copy = pltpu.make_async_copy(
+            ov.at[pl.ds(r0, n)], o_ref.at[pl.ds(r0, n)], lsem.at[8 + 2 * len(CHUNKS) + len(out_copies)]
+        )
+        copy.start()
+        out_copies.append(copy)
+
+    count = len(CHUNKS)
+
+    def step(what, ci):
+        if 0 <= ci < count:
+            what(ci)
+
+    for i in range(count):
+        kv_first(i)
+    make_table()
+    q_copy.wait()
+    for i in range(count):
+        kv_second(i)
+    for i in range(count):
+        kv_share(i)
+        step(x_forward, i - 2)
+        kv_ready(i)
+        attend_chunk(i)
+        x_send(i)
     for w in w_copies:
         w.wait()
-    project(0, 0, 128, start=True)
-    x_forward(2)
-    project(0, 128, 128, start=True)
-    x_near(0)
-    x_near(1)
+    project(0, 0, 256, start=True)
+    x_forward(count - 2)
+    half = 2
+    for i in range(half):
+        x_near(i)
     project(1, 0, 128)
-    x_forward(3)
+    x_forward(count - 1)
     project(2, 0, 128)
-    x_far(0)
-    x_far(1)
+    for i in range(half):
+        x_far(i)
     project(3, 0, 128)
-    x_near(2)
-    x_near(3)
+    put_out(0, 128)
+    for i in range(half, count):
+        x_near(i)
     project(1, 128, 128)
     project(2, 128, 128)
-    x_far(2)
-    x_far(3)
+    for i in range(half, count):
+        x_far(i)
     project(3, 128, 128)
-    o_ref[...] = acc[...].astype(jnp.bfloat16)
+    put_out(128, 128)
+    for copy in out_copies:
+        copy.wait()
     for r in pending:
         r.wait_send()
 
@@ -291,8 +327,8 @@
     return pl.pallas_call(
         attention_kernel,
         out_shape=jax.ShapeDtypeStruct((ROWS, COLS), jnp.bfloat16),
-        in_specs=[anywhere, anywhere, anywhere, pl.BlockSpec(memory_space=pltpu.SMEM), anywhere],
-        out_specs=pl.BlockSpec(memory_space=pltpu.VMEM),
+        in_specs=[anywhere] * 5,
+        out_specs=anywhere,
         scratch_shapes=[
             pltpu.VMEM((ROWS, COLS), jnp.bfloat16),
             gathered,
@@ -300,10 +336,12 @@
             pltpu.VMEM((4, ROWS, COLS), jnp.bfloat16),
             pltpu.VMEM((4, COLS, COLS), jnp.bfloat16),
             pltpu.VMEM((ROWS, COLS), jnp.float32),
+            pltpu.VMEM((ROWS, COLS), jnp.bfloat16),
+            pltpu.SMEM((16,), jnp.int32),
             pltpu.SMEM((32,), jnp.int32),
             pltpu.SemaphoreType.DMA((N_SEM,)),
             pltpu.SemaphoreType.DMA((N_SEM,)),
-            pltpu.SemaphoreType.DMA((16,)),
+            pltpu.SemaphoreType.DMA((16 + 2 * len(CHUNKS),)),
         ],
         compiler_params=pltpu.CompilerParams(
             collective_id=0, has_side_effects=True, vmem_limit_bytes=56 << 20

time: 47.6 us -> 44.3 us (0.931); the launches traced: 46.8 us -> 44.2 us
  Pallas kernels: 45 us -> 42.4 us
    pallas_call x1, Pallas kernels: 45 us -> 42.4 us  [on_device(): pl.pallas_call(attention_kernel, out_shape=jax.ShapeDtypeStruct((ROWS, CO...]
where the time goes in v2:
time: 44.3 us; the launch traced here: 44.2 us
  Pallas kernels  42.4 us (96%)
  local copies, waits for them, and re-layouts  1.82 us (4%)
    pallas_call x1, Pallas kernels, on_device(): pl.pallas_call(attention_kernel, out_shape=jax.ShapeDtypeStruct((ROWS, CO...  42.4 us
    unnamed x1, local copies, waits for them, and re-layouts  1.82 us

profile of v2, /device:TPU:1, one launch (start us, length us, event | category | flops | bytes accessed | tf_op | source)
XLA Modules:
  0.0 44.2 jit_solution(73414282827642555)
XLA Ops:
  0.0 42.4 %shard_map.55 = bf16[256,896]{1,0:T(8,128)(2,1)} custom-call(bf16[256,896]{1,0:T(8,128)(2,1)} %q_ref.1, bf16[256,128]{1,0:T(8,128)(2,1)} %k_ref.1, bf16[256,128]{1,0:T(8,128)(2,1)} %v_ref.1, s32[16]{0:T(128)} %gs_ref.1, bf16[3584,896]{1,0:T(8,128)(2,1)} %w_ref.1), custom_call_target="tpu_custom_call" | custom-call | tf_op jit(solution)/shard_map/pallas_call | solution.py:327
  42.4 1.8 %copy.7 = bf16[256,896]{1,0:T(8,128)(2,1)} copy(bf16[256,896]{1,0:T(8,128)(2,1)} %shard_map.55) | data formatting | bytes 917504

commit v3 on v2

--- a/solution.py
+++ b/solution.py
@@ -13,8 +13,14 @@
 KEYS = 512
 LOG2E = 1.4426950408889634
 QUAD = 32
-CHUNKS = ((0, 64), (64, 64), (128, 64), (192, 64))
-N_SEM = 26 * len(CHUNKS)
+CHUNK_ROWS = (64, 64, 64, 64)
+CHUNKS = tuple((sum(CHUNK_ROWS[:i]), n) for i, n in enumerate(CHUNK_ROWS))
+KV_RELAY = (0, 0, 1, 1)
+X_RELAY = (1, 1, 1, 1)
+TAIL = 1
+UNIT_ROWS = (64, 64, 64, 64)
+UNITS = tuple((sum(UNIT_ROWS[:i]), n) for i, n in enumerate(UNIT_ROWS))
+N_SEM = 24 * len(CHUNKS) + 6 * len(UNITS)
 SCALE = LOG2E * FEAT**-0.5
 NT = (((1,), (1,)), ((), ()))
 
@@ -110,7 +116,7 @@
         r0, n = CHUNKS[ci]
         for t in "kv":
             f, to = firsts(t)
-            for i in range(3):
+            for i in (2, 0, 1):
                 send((t, ci, "f", i), src[t].at[pl.ds(r0, n)], shard(t, f, r0, n), to[i])
             own_copy(t, ci).start()
 
@@ -123,18 +129,45 @@
                 recv((t, ci, "f", i), shard(t, nxt(f, d), r0, n))
             own_copy(t, ci).wait()
             mine = line(t, s, c, r0, n)
-            for i in range(3):
+            for i in (0, 1) if KV_RELAY[ci] else (2, 0, 1):
                 send((t, ci, "s", i), mine, mine, to[i])
             send((t, ci, "c", 3), mine, mine, sibling)
 
+    def kv_share_one(t, ci, i):
+        r0, n = CHUNKS[ci]
+        s, _ = seconds(t)
+        got = line(t, nxt(s, (3, 1, 2)[i]), c, r0, n)
+        send((t, ci, "c", i), got, got, sibling)
+
+    def half_line(t, s, half, r0, n):
+        if t == "k":
+            return kb.at[s, pl.ds(2 * half, 2), c, pl.ds(r0, n)]
+        return vb.at[pl.ds(2 * half, 2), s, c, pl.ds(r0, n)]
+
+    def kv_relay(ci):
+        r0, n = CHUNKS[ci]
+        for i, d in enumerate((3, 1)):
+            for t in "kv":
+                s, to = seconds(t)
+                recv((t, ci, "s", i), line(t, nxt(s, d), c, r0, n))
+                if KV_RELAY[ci]:
+                    part = half_line(t, nxt(s, d), i, r0, n)
+                    send((t, ci, "g", i), part, part, to[i])
+        for i in range(2):
+            for t in "kv":
+                kv_share_one(t, ci, i)
+
     def kv_share(ci):
         r0, n = CHUNKS[ci]
-        for i, d in enumerate((3, 1, 2)):
-            for t in "kv":
-                s, _ = seconds(t)
-                got = line(t, nxt(s, d), c, r0, n)
-                recv((t, ci, "s", i), got)
-                send((t, ci, "c", i), got, got, sibling)
+        for t in "kv":
+            s, _ = seconds(t)
+            far = nxt(s, 2)
+            if KV_RELAY[ci]:
+                for i in range(2):
+                    recv((t, ci, "g", i), half_line(t, far, i, r0, n))
+            else:
+                recv((t, ci, "s", 2), line(t, far, c, r0, n))
+            kv_share_one(t, ci, 2)
 
     def kv_ready(ci):
         r0, n = CHUNKS[ci]
@@ -144,7 +177,7 @@
                 recv((t, ci, "c", i), line(t, nxt(s, d), 1 - c, r0, n))
 
     def halves(ci):
-        r0, n = CHUNKS[ci]
+        r0, n = UNITS[ci]
         return pl.ds(r0, n // 2), pl.ds(r0 + n // 2, n // 2)
 
     def x_send(ci):
@@ -154,14 +187,19 @@
         send(("x", ci, "lb"), xa.at[0, b], xa.at[2, b], left)
         send(("x", ci, "rb"), xa.at[0, b], xa.at[1, b], right)
         send(("x", ci, "la"), xa.at[0, a], xa.at[2, a], left)
+        if not X_RELAY[ci]:
+            both = pl.ds(*UNITS[ci])
+            send(("x", ci, "far"), xa.at[0, both], xa.at[3, both], along_x[2])
 
     def x_forward(ci):
         a, b = halves(ci)
         right, left, _ = along_x
         recv(("x", ci, "ra"), xa.at[1, a])
-        send(("x", ci, "fa"), xa.at[1, a], xa.at[3, a], right)
+        if X_RELAY[ci]:
+            send(("x", ci, "fa"), xa.at[1, a], xa.at[3, a], right)
         recv(("x", ci, "lb"), xa.at[2, b])
-        send(("x", ci, "fb"), xa.at[2, b], xa.at[3, b], left)
+        if X_RELAY[ci]:
+            send(("x", ci, "fb"), xa.at[2, b], xa.at[3, b], left)
 
     def x_near(ci):
         a, b = halves(ci)
@@ -170,10 +208,14 @@
 
     def x_far(ci):
         a, b = halves(ci)
-        recv(("x", ci, "fa"), xa.at[3, a])
-        recv(("x", ci, "fb"), xa.at[3, b])
+        if X_RELAY[ci]:
+            recv(("x", ci, "fa"), xa.at[3, a])
+            recv(("x", ci, "fb"), xa.at[3, b])
+        else:
+            recv(("x", ci, "far"), xa.at[3, pl.ds(*UNITS[ci])])
 
     def make_table():
+        q_copy.wait()
         size_copy.wait()
         listed = [sizes[i] for i in range(16)]
 
@@ -253,11 +295,6 @@
                 at = i * m + h * PAIR
                 xa[0, pair_rows(p), h * FEAT : (h + 1) * FEAT] = out[at : at + PAIR]
 
-    def attend_chunk(ci):
-        r0, n = CHUNKS[ci]
-        for t in range(r0 // QUAD, (r0 + n) // QUAD):
-            attend(t)
-
     def project(slot, r0, n, start=False):
         part = jnp.dot(xa[slot, r0 : r0 + n], wv[slot], preferred_element_type=jnp.float32)
         if start:
@@ -275,46 +312,81 @@
         copy.start()
         out_copies.append(copy)
 
-    count = len(CHUNKS)
-
-    def step(what, ci):
-        if 0 <= ci < count:
-            what(ci)
-
-    for i in range(count):
-        kv_first(i)
+    last = len(UNITS) - TAIL
+    r0 = UNITS[last][0]
+    n = ROWS - r0
+
+    def own_part():
+        for w in w_copies:
+            w.wait()
+        project(0, 0, 256, start=True)
+
+    def near_part():
+        for i in range(last):
+            x_near(i)
+        project(1, 0, r0)
+        project(2, 0, r0)
+
+    def far_part():
+        for i in range(last):
+            x_far(i)
+        project(3, 0, r0)
+        put_out(0, r0)
+
+    def near_last():
+        for i in range(last, len(UNITS)):
+            x_near(i)
+        project(1, r0, n)
+        project(2, r0, n)
+
+    def far_last():
+        for i in range(last, len(UNITS)):
+            x_far(i)
+        project(3, r0, n)
+        put_out(r0, n)
+
+    kv_first(0)
+    kv_first(1)
+    kv_first(2)
+    kv_first(3)
     make_table()
-    q_copy.wait()
-    for i in range(count):
-        kv_second(i)
-    for i in range(count):
-        kv_share(i)
-        step(x_forward, i - 2)
-        kv_ready(i)
-        attend_chunk(i)
-        x_send(i)
-    for w in w_copies:
-        w.wait()
-    project(0, 0, 256, start=True)
-    x_forward(count - 2)
-    half = 2
-    for i in range(half):
-        x_near(i)
-    project(1, 0, 128)
-    x_forward(count - 1)
-    project(2, 0, 128)
-    for i in range(half):
-        x_far(i)
-    project(3, 0, 128)
-    put_out(0, 128)
-    for i in range(half, count):
-        x_near(i)
-    project(1, 128, 128)
-    project(2, 128, 128)
-    for i in range(half, count):
-        x_far(i)
-    project(3, 128, 128)
-    put_out(128, 128)
+    kv_second(0)
+    kv_second(1)
+    kv_second(2)
+    kv_second(3)
+    kv_relay(0)
+    kv_share(0)
+    kv_ready(0)
+    attend(0)
+    attend(1)
+    x_send(0)
+    kv_relay(1)
+    kv_share(1)
+    kv_relay(2)
+    kv_ready(1)
+    attend(2)
+    kv_relay(3)
+    attend(3)
+    x_send(1)
+    kv_share(2)
+    x_forward(0)
+    kv_ready(2)
+    attend(4)
+    attend(5)
+    x_send(2)
+    kv_share(3)
+    x_forward(1)
+    kv_ready(3)
+    attend(6)
+    attend(7)
+    x_send(3)
+    x_forward(2)
+    own_part()
+    x_forward(3)
+    near_part()
+    far_part()
+    near_last()
+    far_last()
     for copy in out_copies:
         copy.wait()
     for r in pending:

time: 44.3 us -> 43.4 us (0.980)
  Pallas kernels: 42.4 us -> 41.4 us
    pallas_call x1, Pallas kernels: 42.4 us -> 41.4 us  [on_device(): pl.pallas_call(attention_kernel, out_shape=jax.ShapeDtypeStruct((ROWS, CO...]
where the time goes in v3:
time: 43.4 us; the launch traced here: 43.2 us
  Pallas kernels  41.4 us (95%)
  local copies, waits for them, and re-layouts  1.82 us (4%)
    pallas_call x1, Pallas kernels, on_device(): pl.pallas_call(attention_kernel, out_shape=jax.ShapeDtypeStruct((ROWS, CO...  41.4 us
    unnamed x1, local copies, waits for them, and re-layouts  1.82 us

profile of v3, /device:TPU:1, one launch (start us, length us, event | category | flops | bytes accessed | tf_op | source)
XLA Modules:
  0.0 43.2 jit_solution(17259145451535663169)
XLA Ops:
  0.0 41.4 %shard_map.55 = bf16[256,896]{1,0:T(8,128)(2,1)} custom-call(bf16[256,896]{1,0:T(8,128)(2,1)} %q_ref.1, bf16[256,128]{1,0:T(8,128)(2,1)} %k_ref.1, bf16[256,128]{1,0:T(8,128)(2,1)} %v_ref.1, s32[16]{0:T(128)} %gs_ref.1, bf16[3584,896]{1,0:T(8,128)(2,1)} %w_ref.1), custom_call_target="tpu_custom_call" | custom-call | tf_op jit(solution)/shard_map/pallas_call | solution.py:399
  41.4 1.8 %copy.7 = bf16[256,896]{1,0:T(8,128)(2,1)} copy(bf16[256,896]{1,0:T(8,128)(2,1)} %shard_map.55) | data formatting | bytes 917504

commit v4 on v3

--- a/solution.py
+++ b/solution.py
@@ -364,8 +364,8 @@
     kv_share(1)
     kv_relay(2)
     kv_ready(1)
+    kv_relay(3)
     attend(2)
-    kv_relay(3)
     attend(3)
     x_send(1)
     kv_share(2)

time: 43.4 us -> 43.3 us (level)
  no operation moved by 1% of the time
where the time goes in v4:
time: 43.3 us; the launch traced here: 43.2 us
  Pallas kernels  41.4 us (96%)
  local copies, waits for them, and re-layouts  1.82 us (4%)
    pallas_call x1, Pallas kernels, on_device(): pl.pallas_call(attention_kernel, out_shape=jax.ShapeDtypeStruct((ROWS, CO...  41.4 us
    unnamed x1, local copies, waits for them, and re-layouts  1.82 us

profile of v4, /device:TPU:1, one launch (start us, length us, event | category | flops | bytes accessed | tf_op | source)
XLA Modules:
  0.0 43.2 jit_solution(15892555909155041926)
XLA Ops:
  0.0 41.4 %shard_map.55 = bf16[256,896]{1,0:T(8,128)(2,1)} custom-call(bf16[256,896]{1,0:T(8,128)(2,1)} %q_ref.1, bf16[256,128]{1,0:T(8,128)(2,1)} %k_ref.1, bf16[256,128]{1,0:T(8,128)(2,1)} %v_ref.1, s32[16]{0:T(128)} %gs_ref.1, bf16[3584,896]{1,0:T(8,128)(2,1)} %w_ref.1), custom_call_target="tpu_custom_call" | custom-call | tf_op jit(solution)/shard_map/pallas_call | solution.py:399
  41.4 1.8 %copy.7 = bf16[256,896]{1,0:T(8,128)(2,1)} copy(bf16[256,896]{1,0:T(8,128)(2,1)} %shard_map.55) | data formatting | bytes 917504
